TPU v7x, 32 devices: a whole 2x2x4 slice. The times are simulated.
32 devices in a mesh: ctx: 8 (over z, core), tp: 4 (over y, x).
Axes of the slice: x: 2, y: 2, z: 4, core: 2. Of those that a mesh axis runs over, the one named last changes fastest.
Arguments:
- query_latent: bfloat16 [4096, 64, 512], P('ctx', 'tp'), may hold values from -24 to 24
- query_rope: bfloat16 [4096, 4096], P('ctx', 'tp'), may hold values from -24 to 24
- key_latent: bfloat16 [4096, 512], P('ctx'), may hold values from -6 to 6
- key_rope: bfloat16 [2048, 128], P('ctx'), may hold values from -6 to 6
- block_ids: int32 [16], replicated, may hold values from 0 to 15, as said below
- value_up: bfloat16 [64, 512, 128], P('tp'), may hold values from -0.5 to 0.5
- out_weight: bfloat16 [8192, 7168], P('tp'), may hold values from -0.0625 to 0.0625
- residual: bfloat16 [4096, 7168], P(('ctx', 'tp')), may hold values from -18 to 18
- norm_gain: float32 [7168], replicated, may hold values from 0.1 to 1.9
- gate_weight: bfloat16 [7168, 2048], P('ctx', 'tp'), may hold values from -0.0625 to 0.0625
- up_weight: bfloat16 [7168, 2048], P('ctx', 'tp'), may hold values from -0.0625 to 0.0625
- down_weight: bfloat16 [7168, 2048], P('ctx', 'tp'), may hold values from -0.125 to 0.125
Outputs:
- layer_out: bfloat16 [4096, 7168], P(('ctx', 'tp'))
Inputs may be any that keep to these rules, and one draw needn't show every extreme that they name: `block_ids`: index c of ctx stores blocks 2c and 2c + 1; their two entries sum to 15, and every value appears once.
All inputs are finite; a program needn't handle non-finite values.
Results may differ from a plain program's by a relative error of at most 0.018.
Values may be sent and summed in bfloat16 or wider, within the bound.
A program may use at most 192 MiB of HBM per device.

v0:
```python
import jax
import jax.numpy as jnp
from jax import lax
from jax.sharding import PartitionSpec as P


def from_behind(x, axis, by):
    length = lax.axis_size(axis)
    return lax.ppermute(x, axis, [(i, (i + by) % length) for i in range(length)])


def rms_norm(activation, gain_vector):
    mean_square = jnp.mean(activation * activation, axis=-1, keepdims=True)
    return (activation * lax.rsqrt(mean_square + 1e-06) * gain_vector).astype(jnp.bfloat16)


def local(
    query_latent,
    query_rope,
    key_latent,
    key_rope,
    block_ids,
    value_up,
    out_weight,
    residual,
    norm_gain,
    gate_weight,
    up_weight,
    down_weight,
):
    seq_rows = key_latent.shape[0]
    half_len = seq_rows // 2
    head_count = query_latent.shape[1]
    rope_dim = key_rope.shape[1] // 2
    head_dim = value_up.shape[2]
    ctx_count = lax.axis_size("ctx")
    tp_count = lax.axis_size("tp")
    score_scale = (head_dim + rope_dim) ** (-0.5)
    recv_latent, recv_rope = from_behind((key_latent, key_rope), "ctx", 1)
    keys_lat = jnp.concatenate([key_latent, recv_latent], axis=0)
    keys_rot = jnp.concatenate(
        [key_rope.reshape(seq_rows, rope_dim), recv_rope.reshape(seq_rows, rope_dim)], axis=0
    )
    current = lax.axis_index("ctx")
    previous = (current + ctx_count - 1) % ctx_count
    own_ids = lax.dynamic_slice_in_dim(block_ids, current * 2, 2, 0)
    prev_ids = lax.dynamic_slice_in_dim(block_ids, previous * 2, 2, 0)
    row_index = jnp.arange(seq_rows, dtype=jnp.int32)
    first_half = row_index < half_len
    offset = row_index % half_len
    query_pos = jnp.where(first_half, own_ids[0], own_ids[1]) * half_len + offset
    key_pos = jnp.concatenate(
        [query_pos, jnp.where(first_half, prev_ids[0], prev_ids[1]) * half_len + offset], axis=0
    )
    rope_queries = query_rope.reshape(seq_rows, head_count, rope_dim)
    block_rows = min(seq_rows, 512)

    def attend(block_index):
        scores = jnp.einsum(
            "shl,kl->hsk", query_latent, keys_lat, preferred_element_type=jnp.float32
        )
        scores = scores + jnp.einsum(
            "shr,kr->hsk", rope_queries, keys_rot, preferred_element_type=jnp.float32
        )
        scores = scores * score_scale
        visible = key_pos[None, :] <= query_pos[:, None]
        scores = jnp.where(visible[None], scores, -jnp.inf)
        highest = jnp.max(scores, axis=-1, keepdims=True)
        exponent = jnp.exp(scores - highest)
        weights = (exponent / jnp.sum(exponent, axis=-1, keepdims=True)).astype(jnp.bfloat16)
        blended = jnp.einsum(
            "hsk,kl->shl", weights, keys_lat, preferred_element_type=jnp.float32
        ).astype(jnp.bfloat16)
        values = jnp.einsum(
            "shl,hlv->shv", blended, value_up, preferred_element_type=jnp.float32
        ).astype(jnp.bfloat16)
        return values.reshape(block_rows, head_count * head_dim)

    head_out = lax.map(attend, jnp.arange(seq_rows // block_rows, dtype=jnp.int32)).reshape(
        seq_rows, head_count * head_dim
    )
    share_rows = seq_rows // tp_count
    tp_index = lax.axis_index("tp")
    partial_attn = jnp.dot(head_out, out_weight, preferred_element_type=jnp.float32)
    attn_total = lax.psum(partial_attn.astype(jnp.bfloat16), "tp").astype(jnp.float32)
    all_residual = lax.all_gather(residual, "tp", axis=0, tiled=True)
    hidden_state = all_residual.astype(jnp.float32) + attn_total
    normed_all = rms_norm(hidden_state, norm_gain)
    own_state = lax.dynamic_slice_in_dim(hidden_state, tp_index * share_rows, share_rows, 0)
    gate_full, up_full, down_full = (
        lax.all_gather(gate_weight, "ctx", axis=0, tiled=True),
        lax.all_gather(up_weight, "ctx", axis=0, tiled=True),
        lax.all_gather(down_weight, "ctx", axis=0, tiled=True),
    )
    gate_proj = jnp.dot(normed_all, gate_full, preferred_element_type=jnp.float32)
    up_proj = jnp.dot(normed_all, up_full, preferred_element_type=jnp.float32)
    hidden_units = (jax.nn.silu(gate_proj) * up_proj).astype(jnp.bfloat16)
    shared_part = lax.psum_scatter(
        lax.dot_general(
            hidden_units, down_full, (((1,), (1,)), ((), ())), preferred_element_type=jnp.float32
        ).astype(jnp.bfloat16),
        "tp",
        scatter_dimension=0,
        tiled=True,
    ).astype(jnp.float32)
    return (own_state + shared_part).astype(jnp.bfloat16)


def solution(mesh):
    placed = (
        P("ctx", "tp", None),
        P("ctx", "tp"),
        P("ctx", None),
        P("ctx", None),
        P(),
        P("tp", None, None),
        P("tp", None),
        P(("ctx", "tp"), None),
        P(),
        P("ctx", "tp"),
        P("ctx", "tp"),
        P("ctx", "tp"),
    )
    return jax.shard_map(
        local, mesh=mesh, in_specs=placed, out_specs=P(("ctx", "tp"), None), check_vma=False
    )
```

profile of v0, /device:TPU:0, one launch (start us, length us, event | category | flops | bytes accessed | tf_op | source)
XLA Modules:
  0.0 672.1 jit_solution(7638917272089841626)
XLA Ops:
  7.0 2.7 collective-permute-start.1
  9.7 0.8 fusion.35
  11.1 1.2 fusion.22
  12.3 1.3 multiply_add_fusion
  13.6 1.2 broadcast_compare_fusion
  14.8 0.9 reshape.69
  15.7 1.5 copy.19
  17.3 1.5 collective-permute-done.1
  19.0 18.1 %fusion.3 = f32[1024,512,16]{1,0,2:T(8,128)} fusion(bf16[512,16,512]{2,1,0:T(8,128)(2,1)} %param.12, bf16[512,512]{1,0:T(8,128)(2,1)} %collective-permute-done, bf16[512,512]{1,0:T(8,128)(2,1)} %param.14), kind=kOutput, calls=%fused_computation.11 | convolution fusion | flops 8592031744 | bytes 42991616 | tf_op jit(solution)/shard_map/while/body/eval_jaxpr/shl,kl->hsk/dot_general | solution.py:59
  37.1 24.3 %fusion.37 = (f32[16,512]{1,0:T(8,128)S(1)}, f32[16,512,1024]{1,2,0:T(8,128)}) fusion(f32[1024,512,16]{1,0,2:T(8,128)} %fusion.3, pred[512,1024]{0,1:T(8,128)(4,1)} %broadcast_compare_fusion, bf16[512,16,64]{0,2,1:T(8,128)(2,1)S(1)} %bitcast.36, bf16[512,64]{0,1:T(8,128)(2,1)S(1)} %copy.18, bf16[512,64]{0,1:T(8,128)(2,1)S(1)} %copy.17), kind=kOutput, calls=%fused_computation.51 | convolution fusion | flops 1115948032 | bytes 68845568 | tf_op jit(solution)/shard_map/while/body/eval_jaxpr/sub | solution.py:69
  61.3 17.5 %fusion.9 = bf16[16,512,128]{1,2,0:T(8,128)(2,1)} fusion(bf16[16,512,128]{2,1,0:T(8,128)(2,1)S(1)} %copy-done, f32[16,512,1024]{1,2,0:T(8,128)} %get-tuple-element.41, f32[16,512]{1,0:T(8,128)S(1)} %get-tuple-element.40, bf16[512,512]{1,0:T(8,128)(2,1)} %collective-permute-done, bf16[512,512]{1,0:T(8,128)(2,1)} %param.14), kind=kOutput, calls=%fused_computation.17 | convolution fusion | flops 9687793664 | bytes 38830080 | tf_op jit(solution)/shard_map/while/body/eval_jaxpr/shl,hlv->shv/dot_general | solution.py:74
  78.9 23.3 %convolution_convert_fusion.1 = bf16[512,7168]{1,0:T(8,128)(2,1)} fusion(bf16[512,2048]{0,1:T(8,128)(2,1)} %bitcast.37, bf16[2048,7168]{1,0:T(8,128)(2,1)} %param.18), kind=kOutput, calls=%fused_computation.10 | convolution fusion | flops 15036055552 | bytes 38797312 | tf_op jit(solution)/shard_map/dot_general | solution.py:84
  102.3 0.7 all-gather.5.cloned.1.call-update
  103.0 0.7 all-gather.7.cloned.1.call-update
  104.9 153.2 %all-reduce.2.cloned.1.call-done = bf16[512,7168]{1,0:T(8,128)(2,1)} async-done(((bf16[512,7168]{1,0:T(8,128)(2,1)}), bf16[512,7168]{1,0:T(8,128)(2,1)}) %all-reduce.2.cloned.1.call-update) | async-done | bytes 7340048 | tf_op jit(solution)/shard_map/psum | solution.py:85
  258.1 80.8 %all-gather.5.cloned.1.call-done = bf16[512,7168]{1,0:T(8,128)(2,1)} async-done(((bf16[128,7168]{1,0:T(8,128)(2,1)}), bf16[512,7168]{1,0:T(8,128)(2,1)}) %all-gather.5.cloned.1.call-update) | async-done | bytes 7340048 | tf_op jit(solution)/shard_map/all_gather | solution.py:86
  338.9 13.5 %convert_add_fusion = (f32[512,7168]{1,0:T(8,128)}, f32[512]{0:T(512)S(1)}) fusion(bf16[512,7168]{1,0:T(8,128)(2,1)} %all-reduce.2.cloned.1.call-done, bf16[512,7168]{1,0:T(8,128)(2,1)} %all-gather.5.cloned.1.call-done), kind=kLoop, calls=%fused_computation.7 | loop fusion | flops 18349568 | bytes 29362176 | tf_op jit(solution)/shard_map/add | solution.py:87
  352.4 61.6 %all-gather.7.cloned.1.call-done = bf16[7168,512]{1,0:T(8,128)(2,1)} async-done(((bf16[896,512]{1,0:T(8,128)(2,1)}), bf16[7168,512]{1,0:T(8,128)(2,1)}) %all-gather.7.cloned.1.call-update) | async-done | bytes 7340048 | tf_op jit(solution)/shard_map/all_gather | solution.py:91
  413.9 9.7 %fusion.33 = f32[512,512]{1,0:T(8,128)S(1)} fusion(bf16[7168,512]{1,0:T(8,128)(2,1)} %all-gather.7.cloned.1.call-done, f32[7168]{0:T(1024)S(1)} %copy-done.2, f32[512]{0:T(512)S(1)} %add_rsqrt_fusion, bf16[512,7168]{1,0:T(8,128)(2,1)} %all-reduce.2.cloned.1.call-done, bf16[512,7168]{1,0:T(8,128)(2,1)} %all-gather.5.cloned.1.call-done), kind=kOutput, calls=%fused_computation.47 | convolution fusion | flops 3780116480 | bytes 23099392 | tf_op jit(solution)/shard_map/dot_general | solution.py:95
  423.7 63.8 %all-gather.11.cloned.1.call-done = bf16[7168,512]{1,0:T(8,128)(2,1)} async-done(((bf16[896,512]{1,0:T(8,128)(2,1)}), bf16[7168,512]{1,0:T(8,128)(2,1)}) %all-gather.11.cloned.1.call-update) | async-done | bytes 7340048 | tf_op jit(solution)/shard_map/all_gather | solution.py:93
  487.5 73.5 %all-gather.9.cloned.1.call-done = bf16[7168,512]{1,0:T(8,128)(2,1)} async-done(((bf16[896,512]{1,0:T(8,128)(2,1)}), bf16[7168,512]{1,0:T(8,128)(2,1)}) %all-gather.9.cloned.1.call-update) | async-done | bytes 7340048 | tf_op jit(solution)/shard_map/all_gather | solution.py:92
  561.0 22.3 %convolution_convert_fusion = bf16[512,7168]{1,0:T(8,128)(2,1)} fusion(bf16[7168,512]{1,0:T(8,128)(2,1)} %all-gather.11.cloned.1.call-done, bf16[7168,512]{1,0:T(8,128)(2,1)} %all-gather.9.cloned.1.call-done, f32[512,512]{1,0:T(8,128)S(1)} %fusion.33, f32[7168]{0:T(1024)S(1)} %copy-done.2, f32[512]{0:T(512)S(1)} %add_rsqrt_fusion, ...), kind=kOutput, calls=%fused_computation.9 | convolution fusion | flops 7543455744 | bytes 37779456 | tf_op jit(solution)/shard_map/dot_general | solution.py:99
  583.3 77.7 %reduce-scatter.2.cloned.1.call-done = bf16[128,7168]{1,0:T(8,128)(2,1)} async-done(((bf16[512,7168]{1,0:T(8,128)(2,1)}), bf16[128,7168]{1,0:T(8,128)(2,1)}) %reduce-scatter.2.cloned.1.call-update) | async-done | bytes 1835024 | tf_op jit(solution)/shard_map/reduce_scatter | solution.py:98
  661.1 4.2 add_convert_fusion
  (24 shorter events, 2.7 us)
Async XLA Ops:
  6.5 54.8 %copy-start = (bf16[16,512,128]{2,1,0:T(8,128)(2,1)S(1)}, bf16[16,512,128]{2,1,0:T(8,128)(2,1)}, u32[]{:S(2)}) copy-start(bf16[16,512,128]{2,1,0:T(8,128)(2,1)} %param.17) | copy-start | bytes 6291460
  6.5 251.6 %all-reduce.2.cloned.1.call-start = ((), (), s32[]{:S(2)}) async-start(), calls=%async_computation.2 | async-start | bytes 14680064 | tf_op jit(solution)/shard_map/psum | solution.py:85
  6.5 12.5 %collective-permute-start = (bf16[512,512]{1,0:T(8,128)(2,1)}, bf16[512,512]{1,0:T(8,128)(2,1)}, u32[]{:S(2)}, u32[]{:S(2)}) collective-permute-start(bf16[512,512]{1,0:T(8,128)(2,1)} %param.14), channel_id=1, source_target_pairs={{0,4},{4,8},{8,12},{12,16},{16,20},{20,24},{24,28},{28,0},{1,5},{5... | collective-permute-start | bytes 1572872 | tf_op jit(solution)/shard_map/ppermute | solution.py:9
  7.0 11.8 %collective-permute-start.1 = (bf16[256,128]{1,0:T(8,128)(2,1)}, bf16[256,128]{1,0:T(8,128)(2,1)S(1)}, u32[]{:S(2)}, u32[]{:S(2)}) collective-permute-start(bf16[256,128]{1,0:T(8,128)(2,1)} %param.15), channel_id=1, source_target_pairs={{0,4},{4,8},{8,12},{12,16},{16,20},{20,24},{24,28},{28,0},{1,5},{5... | collective-permute-start | bytes 196616 | tf_op jit(solution)/shard_map/ppermute | solution.py:9
  102.2 236.6 %all-gather.5.cloned.1.call-start = ((), (), s32[]{:S(2)}) async-start(), calls=%async_computation.1 | async-start | bytes 9175040 | tf_op jit(solution)/shard_map/all_gather | solution.py:86
  103.0 311.0 %all-gather.7.cloned.1.call-start = ((), (), s32[]{:S(2)}) async-start(), calls=%async_computation.3 | async-start | bytes 8257536 | tf_op jit(solution)/shard_map/all_gather | solution.py:91
  103.7 383.8 %all-gather.11.cloned.1.call-start = ((), (), s32[]{:S(2)}) async-start(), calls=%async_computation.5 | async-start | bytes 8257536 | tf_op jit(solution)/shard_map/all_gather | solution.py:93
  104.3 456.7 %all-gather.9.cloned.1.call-start = ((), (), s32[]{:S(2)}) async-start(), calls=%async_computation.4 | async-start | bytes 8257536 | tf_op jit(solution)/shard_map/all_gather | solution.py:92
  104.9 309.1 %copy-start.2 = (f32[7168]{0:T(1024)S(1)}, f32[7168]{0:T(1024)}, u32[]{:S(2)}) copy-start(f32[7168]{0:T(1024)} %param.20) | copy-start | bytes 86020
  104.9 556.2 %reduce-scatter.2.cloned.1.call-start = ((), (), s32[]{:S(2)}) async-start(), calls=%async_computation.6 | async-start | bytes 9175040 | tf_op jit(solution)/shard_map/reduce_scatter | solution.py:98
  583.3 81.9 %copy-start.1 = (bf16[16,512,128]{2,1,0:T(8,128)(2,1)S(1)}, bf16[16,512,128]{2,1,0:T(8,128)(2,1)}, u32[]{:S(2)}) copy-start(bf16[16,512,128]{2,1,0:T(8,128)(2,1)} %param.17) | copy-start | bytes 6291460
Sparse Core Ops, SparseCore 0:
  102.3 155.7 all-reduce.1
  259.9 78.8 all-gather.4
  340.5 73.3 all-gather.6
  415.4 71.9 all-gather.10
  489.0 71.9 all-gather.8
  583.5 77.5 reduce-scatter.1
where the time goes:
time: 672 us
  waiting for transfers between devices  515 us (77%)
  matrix products  115 us (17%)
  other arithmetic  21.3 us (3%)
  between operations  13.6 us (2%)
    psum x1, waiting for transfers between devices, local(): lax.psum(partial_attn.astype(jnp.bfloat16), 'tp').astype(jnp.float32)  153 us
    all_gather x1, waiting for transfers between devices, local(): all_residual = lax.all_gather(residual, 'tp', axis=0, tiled=True)  80.8 us
    reduce_scatter x1, waiting for transfers between devices, local(): lax.psum_scatter(lax.dot_general(hidden_units, down_full, (((1,), (1,)),...  77.7 us
    all_gather x1, waiting for transfers between devices, local(): lax.all_gather(up_weight, 'ctx', axis=0, tiled=True)  73.5 us
    all_gather x1, waiting for transfers between devices, local(): lax.all_gather(down_weight, 'ctx', axis=0, tiled=True)  63.8 us
    all_gather x1, waiting for transfers between devices, local(): lax.all_gather(gate_weight, 'ctx', axis=0, tiled=True)  61.6 us
    sub x1, matrix products, attend(): exponent = jnp.exp(scores - highest)  24.3 us
    dot_general x1, matrix products, local(): jnp.dot(head_out, out_weight, preferred_element_type=jnp.float32)  23.3 us
  transfers between devices with their start and end apart: 8, of which 7 were waited for; matrix products, arithmetic and copies ran while one was open for 5% of the time, Pallas kernels for 0%

commit v1 on v0

--- a/solution.py
+++ b/solution.py
@@ -2,6 +2,25 @@
 import jax.numpy as jnp
 from jax import lax
 from jax.sharding import PartitionSpec as P
+
+
+def gather_around(x, axis, dim):
+    size, index, rows = (lax.axis_size(axis), lax.axis_index(axis), x.shape[dim])
+    ahead = [(i, (i + 1) % size) for i in range(size)]
+    downward = [(i, (i - 1) % size) for i in range(size)]
+    out = jnp.zeros((*x.shape[:dim], size * rows, *x.shape[dim + 1 :]), x.dtype)
+    out = lax.dynamic_update_slice_in_dim(out, x, index * rows, axis=dim)
+    from_left = from_right = x
+    half = size // 2
+    for lap in range(1, half + 1):
+        from_left = lax.ppermute(from_left, axis, ahead)
+        out = lax.dynamic_update_slice_in_dim(out, from_left, (index - lap) % size * rows, axis=dim)
+        if lap < size - half:
+            from_right = lax.ppermute(from_right, axis, downward)
+            out = lax.dynamic_update_slice_in_dim(
+                out, from_right, (index + lap) % size * rows, axis=dim
+            )
+    return out
 
 
 def from_behind(x, axis, by):
@@ -88,7 +107,7 @@
     normed_all = rms_norm(hidden_state, norm_gain)
     own_state = lax.dynamic_slice_in_dim(hidden_state, tp_index * share_rows, share_rows, 0)
     gate_full, up_full, down_full = (
-        lax.all_gather(gate_weight, "ctx", axis=0, tiled=True),
+        gather_around(gate_weight, "ctx", 0),
         lax.all_gather(up_weight, "ctx", axis=0, tiled=True),
         lax.all_gather(down_weight, "ctx", axis=0, tiled=True),
     )

time: 672 us -> 599 us (0.89)
  waiting for transfers between devices: 515 us -> 414 us
  local copies, waits for them, and re-layouts: 4.16 us -> 20.7 us
  starting transfers between devices: 3.33 us -> 14 us
    psum x1, waiting for transfers between devices: 153 us -> 66.8 us  [local(): lax.psum(partial_attn.astype(jnp.bfloat16), 'tp').astype(jnp.float32)]
    all_gather x1 -> x0, waiting for transfers between devices: 61.6 us -> none  [local(): lax.all_gather(gate_weight, 'ctx', axis=0, tiled=True)]
    ppermute x0 -> x7, waiting for transfers between devices: none -> 59.7 us  [the longest x4 59.7 us: gather_around(): from_left = lax.ppermute(from_left, axis, ahead)]
    dynamic_update_slice x0 -> x8, local copies, waits for them, and re-layouts: none -> 13 us  [the longest x4 6.5 us: gather_around(): lax.dynamic_update_slice_in_dim(out, from_left, (index - lap) % size * ro...]
    all_gather x1, waiting for transfers between devices: 73.5 us -> 61.6 us  [local(): lax.all_gather(up_weight, 'ctx', axis=0, tiled=True)]
    ppermute x0 -> x7, starting transfers between devices: none -> 10.7 us  [the longest x3 10.6 us: gather_around(): from_right = lax.ppermute(from_right, axis, downward)]
  transfers between devices with their start and end apart: 8 -> 14, of which waited for: 7 -> 9; matrix products, arithmetic and copies ran while one was open for 5% -> 8% of each run, Pallas kernels for 0% -> 0%
where the time goes in v1:
time: 599 us; the launch traced here: 598 us
  waiting for transfers between devices  414 us (69%)
  matrix products  115 us (19%)
  other arithmetic  21.4 us (4%)
  local copies, waits for them, and re-layouts  20.7 us (3%)
  starting transfers between devices  14 us (2%)
  between operations  13.3 us (2%)
    all_gather x1, waiting for transfers between devices, local(): all_residual = lax.all_gather(residual, 'tp', axis=0, tiled=True)  80.8 us
    reduce_scatter x1, waiting for transfers between devices, local(): lax.psum_scatter(lax.dot_general(hidden_units, down_full, (((1,), (1,)),...  77.7 us
    psum x1, waiting for transfers between devices, local(): lax.psum(partial_attn.astype(jnp.bfloat16), 'tp').astype(jnp.float32)  66.8 us
    all_gather x1, waiting for transfers between devices, local(): lax.all_gather(down_weight, 'ctx', axis=0, tiled=True)  63.8 us
    all_gather x1, waiting for transfers between devices, local(): lax.all_gather(up_weight, 'ctx', axis=0, tiled=True)  61.6 us
    ppermute x4, waiting for transfers between devices, gather_around(): from_left = lax.ppermute(from_left, axis, ahead)  59.7 us
    sub x1, matrix products, attend(): exponent = jnp.exp(scores - highest)  24.3 us
    dot_general x1, matrix products, local(): jnp.dot(head_out, out_weight, preferred_element_type=jnp.float32)  23.3 us
  transfers between devices with their start and end apart: 14, of which 9 were waited for; matrix products, arithmetic and copies ran while one was open for 8% of the time, Pallas kernels for 0%

profile of v1, /device:TPU:0, one launch (start us, length us, event | category | flops | bytes accessed | tf_op | source)
XLA Modules:
  0.0 598.3 jit_solution(13329576980836910883)
XLA Ops:
  7.0 2.7 collective-permute-start.1
  19.0 18.0 %fusion.3 = f32[1024,512,16]{1,0,2:T(8,128)} fusion(bf16[512,16,512]{2,1,0:T(8,128)(2,1)} %param.12, bf16[512,512]{1,0:T(8,128)(2,1)} %collective-permute-done, bf16[512,512]{1,0:T(8,128)(2,1)} %param.14), kind=kOutput, calls=%fused_computation.11 | convolution fusion | flops 8592031744 | bytes 42991616 | tf_op jit(solution)/shard_map/while/body/eval_jaxpr/shl,kl->hsk/dot_general | solution.py:78
  37.1 24.3 %fusion.32 = (f32[16,512]{1,0:T(8,128)S(1)}, f32[16,512,1024]{1,2,0:T(8,128)}) fusion(f32[1024,512,16]{1,0,2:T(8,128)} %fusion.3, pred[512,1024]{0,1:T(8,128)(4,1)} %broadcast_compare_fusion, bf16[512,16,64]{0,2,1:T(8,128)(2,1)S(1)} %bitcast.36, bf16[512,64]{0,1:T(8,128)(2,1)S(1)} %copy.18, bf16[512,64]{0,1:T(8,128)(2,1)S(1)} %copy.17), kind=kOutput, calls=%fused_computation.54 | convolution fusion | flops 1115948032 | bytes 68845568 | tf_op jit(solution)/shard_map/while/body/eval_jaxpr/sub | solution.py:88
  61.3 17.5 %fusion.9 = bf16[16,512,128]{1,2,0:T(8,128)(2,1)} fusion(bf16[16,512,128]{2,1,0:T(8,128)(2,1)S(1)} %copy-done, f32[16,512,1024]{1,2,0:T(8,128)} %get-tuple-element.41, f32[16,512]{1,0:T(8,128)S(1)} %get-tuple-element.40, bf16[512,512]{1,0:T(8,128)(2,1)} %collective-permute-done, bf16[512,512]{1,0:T(8,128)(2,1)} %param.14), kind=kOutput, calls=%fused_computation.17 | convolution fusion | flops 9687793664 | bytes 38830080 | tf_op jit(solution)/shard_map/while/body/eval_jaxpr/shl,hlv->shv/dot_general | solution.py:93
  78.9 23.3 %convolution_convert_fusion.1 = bf16[512,7168]{1,0:T(8,128)(2,1)} fusion(bf16[512,2048]{0,1:T(8,128)(2,1)} %bitcast.37, bf16[2048,7168]{1,0:T(8,128)(2,1)} %param.18), kind=kOutput, calls=%fused_computation.10 | convolution fusion | flops 15036055552 | bytes 38797312 | tf_op jit(solution)/shard_map/dot_general | solution.py:103
  104.4 3.5 collective-permute-start.3
  107.9 20.1 %collective-permute-done.2 = bf16[896,512]{1,0:T(8,128)(2,1)S(1)} collective-permute-done((bf16[896,512]{1,0:T(8,128)(2,1)S(1)}, bf16[896,512]{1,0:T(8,128)(2,1)S(1)}, u32[]{:S(2)}, u32[]{:S(2)}) %collective-permute-start.2) | collective-permute-done | bytes 917536 | tf_op jit(solution)/shard_map/ppermute | solution.py:16
  128.0 3.5 collective-permute-start.5
  131.5 20.4 %collective-permute-done.4 = bf16[896,512]{1,0:T(8,128)(2,1)} collective-permute-done((bf16[896,512]{1,0:T(8,128)(2,1)S(1)}, bf16[896,512]{1,0:T(8,128)(2,1)}, u32[]{:S(2)}, u32[]{:S(2)}) %collective-permute-start.4) | collective-permute-done | bytes 917536 | tf_op jit(solution)/shard_map/ppermute | solution.py:16
  152.0 3.5 collective-permute-start.7
  155.5 19.2 %collective-permute-done.6 = bf16[896,512]{1,0:T(8,128)(2,1)} collective-permute-done((bf16[896,512]{1,0:T(8,128)(2,1)}, bf16[896,512]{1,0:T(8,128)(2,1)}, u32[]{:S(2)}, u32[]{:S(2)}) %collective-permute-start.6) | collective-permute-done | bytes 917536 | tf_op jit(solution)/shard_map/ppermute | solution.py:16
  174.7 3.5 broadcast_in_dim.55
  181.1 2.2 constant_dynamic-update-slice_fusion.4
  185.5 2.3 constant_dynamic-update-slice_fusion.2
  187.8 2.4 constant_dynamic-update-slice_fusion.1
  191.2 66.8 %all-reduce.2.cloned.1.call-done = bf16[512,7168]{1,0:T(8,128)(2,1)} async-done(((bf16[512,7168]{1,0:T(8,128)(2,1)}), bf16[512,7168]{1,0:T(8,128)(2,1)}) %all-reduce.2.cloned.1.call-update) | async-done | bytes 7340048 | tf_op jit(solution)/shard_map/psum | solution.py:104
  258.1 80.8 %all-gather.4.cloned.1.call-done = bf16[512,7168]{1,0:T(8,128)(2,1)} async-done(((bf16[128,7168]{1,0:T(8,128)(2,1)}), bf16[512,7168]{1,0:T(8,128)(2,1)}) %all-gather.4.cloned.1.call-update) | async-done | bytes 7340048 | tf_op jit(solution)/shard_map/all_gather | solution.py:105
  338.8 13.5 %convert_add_fusion = (f32[512,7168]{1,0:T(8,128)}, f32[512]{0:T(512)S(1)}) fusion(bf16[512,7168]{1,0:T(8,128)(2,1)} %all-reduce.2.cloned.1.call-done, bf16[512,7168]{1,0:T(8,128)(2,1)} %all-gather.4.cloned.1.call-done), kind=kLoop, calls=%fused_computation.7 | loop fusion | flops 18349568 | bytes 29362176 | tf_op jit(solution)/shard_map/add | solution.py:106
  352.3 61.6 %all-gather.6.cloned.1.call-done = bf16[7168,512]{1,0:T(8,128)(2,1)} async-done(((bf16[896,512]{1,0:T(8,128)(2,1)}), bf16[7168,512]{1,0:T(8,128)(2,1)}) %all-gather.6.cloned.1.call-update) | async-done | bytes 7340048 | tf_op jit(solution)/shard_map/all_gather | solution.py:111
  413.9 9.7 %fusion.27 = f32[512,512]{1,0:T(8,128)S(1)} fusion(bf16[7168,512]{1,0:T(8,128)(2,1)} %all-gather.6.cloned.1.call-done, f32[7168]{0:T(1024)S(1)} %copy-done.3, f32[512]{0:T(512)S(1)} %add_rsqrt_fusion, bf16[512,7168]{1,0:T(8,128)(2,1)} %all-reduce.2.cloned.1.call-done, bf16[512,7168]{1,0:T(8,128)(2,1)} %all-gather.4.cloned.1.call-done), kind=kOutput, calls=%fused_computation.49 | convolution fusion | flops 3780116480 | bytes 23099392 | tf_op jit(solution)/shard_map/dot_general | solution.py:115
  423.6 63.8 %all-gather.8.cloned.1.call-done = bf16[7168,512]{1,0:T(8,128)(2,1)} async-done(((bf16[896,512]{1,0:T(8,128)(2,1)}), bf16[7168,512]{1,0:T(8,128)(2,1)}) %all-gather.8.cloned.1.call-update) | async-done | bytes 7340048 | tf_op jit(solution)/shard_map/all_gather | solution.py:112
  487.4 22.4 %convolution_convert_fusion = bf16[512,7168]{1,0:T(8,128)(2,1)} fusion(bf16[7168,512]{1,0:T(8,128)(2,1)} %all-gather.8.cloned.1.call-done, f32[512,512]{1,0:T(8,128)S(1)} %fusion.27, bf16[7168,512]{1,0:T(8,128)(2,1)} %constant_dynamic-update-slice_fusion, f32[7168]{0:T(1024)S(1)} %copy-done.3, f32[512]{0:T(512)S(1)} %add_rsqrt_fusion, ...), kind=kOutput, calls=%fused_computation.9 | convolution fusion | flops 7543455744 | bytes 37779456 | tf_op jit(solution)/shard_map/dot_general | solution.py:118
  509.9 77.7 %reduce-scatter.2.cloned.1.call-done = bf16[128,7168]{1,0:T(8,128)(2,1)} async-done(((bf16[512,7168]{1,0:T(8,128)(2,1)}), bf16[128,7168]{1,0:T(8,128)(2,1)}) %reduce-scatter.2.cloned.1.call-update) | async-done | bytes 1835024 | tf_op jit(solution)/shard_map/reduce_scatter | solution.py:117
  587.6 4.2 add_convert_fusion
  (46 shorter events, 18.1 us)
Async XLA Ops:
  6.5 54.8 %copy-start = (bf16[16,512,128]{2,1,0:T(8,128)(2,1)S(1)}, bf16[16,512,128]{2,1,0:T(8,128)(2,1)}, u32[]{:S(2)}) copy-start(bf16[16,512,128]{2,1,0:T(8,128)(2,1)} %param.17) | copy-start | bytes 6291460
  6.5 251.5 %all-reduce.2.cloned.1.call-start = ((), (), s32[]{:S(2)}) async-start(), calls=%async_computation.2 | async-start | bytes 14680064 | tf_op jit(solution)/shard_map/psum | solution.py:104
  6.5 12.5 %collective-permute-start = (bf16[512,512]{1,0:T(8,128)(2,1)}, bf16[512,512]{1,0:T(8,128)(2,1)}, u32[]{:S(2)}, u32[]{:S(2)}) collective-permute-start(bf16[512,512]{1,0:T(8,128)(2,1)} %param.14), channel_id=1, source_target_pairs={{0,4},{4,8},{8,12},{12,16},{16,20},{20,24},{24,28},{28,0},{1,5},{5... | collective-permute-start | bytes 1572872 | tf_op jit(solution)/shard_map/ppermute | solution.py:28
  7.0 11.8 %collective-permute-start.1 = (bf16[256,128]{1,0:T(8,128)(2,1)}, bf16[256,128]{1,0:T(8,128)(2,1)S(1)}, u32[]{:S(2)}, u32[]{:S(2)}) collective-permute-start(bf16[256,128]{1,0:T(8,128)(2,1)} %param.15), channel_id=1, source_target_pairs={{0,4},{4,8},{8,12},{12,16},{16,20},{20,24},{24,28},{28,0},{1,5},{5... | collective-permute-start | bytes 196616 | tf_op jit(solution)/shard_map/ppermute | solution.py:28
  102.2 2.1 copy-start.2
  102.2 236.6 %all-gather.4.cloned.1.call-start = ((), (), s32[]{:S(2)}) async-start(), calls=%async_computation.1 | async-start | bytes 9175040 | tf_op jit(solution)/shard_map/all_gather | solution.py:105
  102.9 311.0 %all-gather.6.cloned.1.call-start = ((), (), s32[]{:S(2)}) async-start(), calls=%async_computation.3 | async-start | bytes 8257536 | tf_op jit(solution)/shard_map/all_gather | solution.py:111
  103.7 383.8 %all-gather.8.cloned.1.call-start = ((), (), s32[]{:S(2)}) async-start(), calls=%async_computation.4 | async-start | bytes 8257536 | tf_op jit(solution)/shard_map/all_gather | solution.py:112
  104.2 483.4 %reduce-scatter.2.cloned.1.call-start = ((), (), s32[]{:S(2)}) async-start(), calls=%async_computation.5 | async-start | bytes 9175040 | tf_op jit(solution)/shard_map/reduce_scatter | solution.py:117
  104.3 23.7 %collective-permute-start.2 = (bf16[896,512]{1,0:T(8,128)(2,1)S(1)}, bf16[896,512]{1,0:T(8,128)(2,1)S(1)}, u32[]{:S(2)}, u32[]{:S(2)}) collective-permute-start(bf16[896,512]{1,0:T(8,128)(2,1)S(1)} %copy-done.2), channel_id=1, source_target_pairs={{0,4},{4,8},{8,12},{12,16},{16,20},{20,24},{24,28},{28,0},{1,5},{5... | collective-permute-start | bytes 2752520 | tf_op jit(solution)/shard_map/ppermute | solution.py:16
  104.4 23.6 %collective-permute-start.3 = (bf16[896,512]{1,0:T(8,128)(2,1)S(1)}, bf16[896,512]{1,0:T(8,128)(2,1)S(1)}, u32[]{:S(2)}, u32[]{:S(2)}) collective-permute-start(bf16[896,512]{1,0:T(8,128)(2,1)S(1)} %copy-done.2), channel_id=1, source_target_pairs={{0,28},{4,0},{8,4},{12,8},{16,12},{20,16},{24,20},{28,24},{1,29},{... | collective-permute-start | bytes 2752520 | tf_op jit(solution)/shard_map/ppermute | solution.py:19
  128.0 24.0 %collective-permute-start.4 = (bf16[896,512]{1,0:T(8,128)(2,1)S(1)}, bf16[896,512]{1,0:T(8,128)(2,1)}, u32[]{:S(2)}, u32[]{:S(2)}) collective-permute-start(bf16[896,512]{1,0:T(8,128)(2,1)S(1)} %collective-permute-done.2), channel_id=1, source_target_pairs={{0,4},{4,8},{8,12},{12,16},{16,20},{20,24},{24,28},{28,0},{1,5},{5... | collective-permute-start | bytes 2752520 | tf_op jit(solution)/shard_map/ppermute | solution.py:16
  128.0 24.0 %collective-permute-start.5 = (bf16[896,512]{1,0:T(8,128)(2,1)S(1)}, bf16[896,512]{1,0:T(8,128)(2,1)}, u32[]{:S(2)}, u32[]{:S(2)}) collective-permute-start(bf16[896,512]{1,0:T(8,128)(2,1)S(1)} %collective-permute-done.3), channel_id=1, source_target_pairs={{0,28},{4,0},{8,4},{12,8},{16,12},{20,16},{24,20},{28,24},{1,29},{... | collective-permute-start | bytes 2752520 | tf_op jit(solution)/shard_map/ppermute | solution.py:19
  152.0 22.7 %collective-permute-start.6 = (bf16[896,512]{1,0:T(8,128)(2,1)}, bf16[896,512]{1,0:T(8,128)(2,1)}, u32[]{:S(2)}, u32[]{:S(2)}) collective-permute-start(bf16[896,512]{1,0:T(8,128)(2,1)} %collective-permute-done.4), channel_id=1, source_target_pairs={{0,4},{4,8},{8,12},{12,16},{16,20},{20,24},{24,28},{28,0},{1,5},{5... | collective-permute-start | bytes 2752520 | tf_op jit(solution)/shard_map/ppermute | solution.py:16
  152.0 35.8 %collective-permute-start.7 = (bf16[896,512]{1,0:T(8,128)(2,1)}, bf16[896,512]{1,0:T(8,128)(2,1)}, u32[]{:S(2)}, u32[]{:S(2)}) collective-permute-start(bf16[896,512]{1,0:T(8,128)(2,1)} %collective-permute-done.5), channel_id=1, source_target_pairs={{0,28},{4,0},{8,4},{12,8},{16,12},{20,16},{24,20},{28,24},{1,29},{... | collective-permute-start | bytes 2752520 | tf_op jit(solution)/shard_map/ppermute | solution.py:19
  174.7 15.5 %collective-permute-start.8 = (bf16[896,512]{1,0:T(8,128)(2,1)}, bf16[896,512]{1,0:T(8,128)(2,1)S(1)}, u32[]{:S(2)}, u32[]{:S(2)}) collective-permute-start(bf16[896,512]{1,0:T(8,128)(2,1)} %collective-permute-done.6), channel_id=1, source_target_pairs={{0,4},{4,8},{8,12},{12,16},{16,20},{20,24},{24,28},{28,0},{1,5},{5... | collective-permute-start | bytes 2752520 | tf_op jit(solution)/shard_map/ppermute | solution.py:16
  191.2 222.7 %copy-start.3 = (f32[7168]{0:T(1024)S(1)}, f32[7168]{0:T(1024)}, u32[]{:S(2)}) copy-start(f32[7168]{0:T(1024)} %param.20) | copy-start | bytes 86020
  509.8 81.9 %copy-start.1 = (bf16[16,512,128]{2,1,0:T(8,128)(2,1)S(1)}, bf16[16,512,128]{2,1,0:T(8,128)(2,1)}, u32[]{:S(2)}) copy-start(bf16[16,512,128]{2,1,0:T(8,128)(2,1)} %param.17) | copy-start | bytes 6291460
Sparse Core Ops, SparseCore 0:
  102.3 155.7 all-reduce.1
  259.9 78.8 all-gather.3
  340.5 73.3 all-gather.5
  415.4 71.9 all-gather.7
  510.0 77.5 reduce-scatter.1
